TPU v7x, 32 devices: a whole 2x2x4 slice. The times are simulated.
32 devices in a mesh: row: 4 (over y, x), col: 8 (over z, core).
Axes of the slice: x: 2, y: 2, z: 4, core: 2. Of those that a mesh axis runs over, the one named last changes fastest.
Arguments:
- pair: bfloat16 [256, 256, 128], P('row', 'col'), may hold values from -6 to 6
- cotangent: bfloat16 [256, 256, 128], P('row', 'col'), may hold values from -6 to 6
- res_mask: int32 [256], replicated, may hold values 0 or 1
- chain: int32 [256], replicated, may hold values from 0 to 3, never falling along the last dimension, each value on 1 to 128 neighbouring positions
- ln_in_gain: float32 [128], replicated, may hold values from 0.5 to 1.5
- ln_in_bias: float32 [128], replicated, may hold values from -3 to 3
- w_proj: bfloat16 [128, 512], replicated, may hold values from -0.5 to 0.5
- w_gate: bfloat16 [128, 128], replicated, may hold values from -0.5 to 0.5
- chain_bias: float32 [128], replicated, may hold values from -4 to 4
- ln_out_gain: float32 [128], replicated, may hold values from 0.5 to 1.5
- ln_out_bias: float32 [128], replicated, may hold values from -3 to 3
- w_out: bfloat16 [128, 128], replicated, may hold values from -0.5 to 0.5
Outputs:
- grad_pair: bfloat16 [256, 256, 128], P('row', 'col')
- grad_proj: float32 [128, 512], replicated
- grad_gate: float32 [128, 128], replicated
- grad_out: float32 [128, 128], replicated
Inputs may be any that keep to these rules, and one draw needn't show every extreme that they name: chain never decreases along the residues.
All inputs are finite; a program needn't handle non-finite values.
Results may differ from a plain program's by a relative error of at most 0.02.
Values may be sent and summed in bfloat16 or wider, within the bound.
A program may use at most 128 MiB of HBM per device.

v0:
```python
import jax
import jax.numpy as jnp
from jax import lax
from jax.sharding import PartitionSpec as P

EPS = 1e-05


def layer_norm(values, gain, bias):
    mean = jnp.mean(values, axis=-1, keepdims=True)
    centred = values - mean
    inverse = lax.rsqrt(jnp.mean(centred * centred, axis=-1, keepdims=True) + EPS)
    normed = centred * inverse
    return (normed * gain + bias, normed, inverse)


def norm_back(grad_normed, normed, inverse):
    first = jnp.mean(grad_normed, axis=-1, keepdims=True)
    second = jnp.mean(grad_normed * normed, axis=-1, keepdims=True)
    return (grad_normed - first - normed * second) * inverse


def matmul_last(left, right):
    shape = left.shape
    flat = jnp.dot(left.reshape(-1, shape[-1]), right, preferred_element_type=jnp.float32)
    return flat.reshape(shape[:-1] + (right.shape[1],))


def contract_pairs(left, right):
    flat_left = left.reshape(-1, left.shape[-1])
    flat_right = right.reshape(-1, right.shape[-1])
    return lax.dot_general(
        flat_left, flat_right, (((0,), (0,)), ((), ())), preferred_element_type=jnp.float32
    )


def project(pair, ln_in_gain, ln_in_bias, w_proj):
    scaled, normed, inverse = layer_norm(pair.astype(jnp.float32), ln_in_gain, ln_in_bias)
    normed_b = scaled.astype(jnp.bfloat16)
    return (normed_b, normed, inverse, matmul_last(normed_b, w_proj))


def activations(proj, pair_mask):
    width = proj.shape[-1] // 4
    gate_a = jax.nn.sigmoid(proj[..., :width])
    gate_b = jax.nn.sigmoid(proj[..., 2 * width : 3 * width])
    act_a = (gate_a * proj[..., width : 2 * width] * pair_mask).astype(jnp.bfloat16)
    act_b = (gate_b * proj[..., 3 * width :] * pair_mask).astype(jnp.bfloat16)
    return (act_a, act_b)


def gated_output(
    mixed, cotangent, normed_b, same, chain_bias, w_gate, ln_out_gain, ln_out_bias, w_out
):
    scaled, normed, inverse = layer_norm(mixed, ln_out_gain, ln_out_bias)
    out_b = scaled.astype(jnp.bfloat16)
    update = matmul_last(out_b, w_out)
    gate = jax.nn.sigmoid(matmul_last(normed_b, w_gate) + same * chain_bias)
    cot = cotangent.astype(jnp.float32)
    grad_update = (cot * gate).astype(jnp.bfloat16)
    grad_logit = (cot * update * gate * (1.0 - gate)).astype(jnp.bfloat16)
    grad_scaled = matmul_last(grad_update, w_out.T)
    grad_mixed = norm_back(grad_scaled * ln_out_gain, normed, inverse).astype(jnp.bfloat16)
    return (
        grad_mixed,
        grad_logit,
        contract_pairs(out_b, grad_update),
        contract_pairs(normed_b, grad_logit),
    )


def input_back(
    normed_b,
    normed,
    inverse,
    proj,
    pair_mask,
    grad_a,
    grad_b,
    grad_logit,
    ln_in_gain,
    w_proj,
    w_gate,
):
    width = proj.shape[-1] // 4
    gate_a = jax.nn.sigmoid(proj[..., :width])
    gate_b = jax.nn.sigmoid(proj[..., 2 * width : 3 * width])
    masked_a = grad_a * pair_mask
    masked_b = grad_b * pair_mask
    grad_p = jnp.concatenate(
        [
            masked_a * proj[..., width : 2 * width] * gate_a * (1.0 - gate_a),
            masked_a * gate_a,
            masked_b * proj[..., 3 * width :] * gate_b * (1.0 - gate_b),
            masked_b * gate_b,
        ],
        axis=-1,
    ).astype(jnp.bfloat16)
    grad_zn = matmul_last(grad_p, w_proj.T) + matmul_last(grad_logit, w_gate.T)
    grad_pair = norm_back(grad_zn * ln_in_gain, normed, inverse).astype(jnp.bfloat16)
    return (grad_pair, contract_pairs(normed_b, grad_p))


def body(
    pair,
    cotangent,
    res_mask,
    chain,
    ln_in_gain,
    ln_in_bias,
    w_proj,
    w_gate,
    chain_bias,
    ln_out_gain,
    ln_out_bias,
    w_out,
):
    tile_rows = pair.shape[0]
    tile_cols = pair.shape[1]
    total = tile_rows * lax.axis_size("row")
    row_start = lax.axis_index("row") * tile_rows
    col_start = lax.axis_index("col") * tile_cols
    maskf = res_mask.astype(jnp.float32)
    mask_rows = lax.dynamic_slice_in_dim(maskf, row_start, tile_rows)
    mask_cols = lax.dynamic_slice_in_dim(maskf, col_start, tile_cols)
    pair_mask = mask_rows[:, None, None] * mask_cols[None, :, None]
    chain_rows = lax.dynamic_slice_in_dim(chain, row_start, tile_rows)
    chain_cols = lax.dynamic_slice_in_dim(chain, col_start, tile_cols)
    same = (chain_rows[:, None] == chain_cols[None, :]).astype(jnp.float32)[:, :, None]
    normed_b, normed, inverse, proj = project(pair, ln_in_gain, ln_in_bias, w_proj)
    act_a, act_b = activations(proj, pair_mask)
    b_cols = lax.all_gather(act_b, "row", axis=0, tiled=True)
    piece = b_cols
    mixed = jnp.transpose(
        lax.psum_scatter(
            jnp.einsum("ikh,jkh->jih", act_a, piece, preferred_element_type=jnp.float32).astype(
                jnp.bfloat16
            ),
            "col",
            scatter_dimension=0,
            tiled=True,
        ).astype(jnp.float32),
        (1, 0, 2),
    )
    grad_mixed, grad_logit, term_out, term_gate = gated_output(
        mixed, cotangent, normed_b, same, chain_bias, w_gate, ln_out_gain, ln_out_bias, w_out
    )
    dx_rows = lax.all_gather(grad_mixed, "col", axis=1, tiled=True)
    grad_a = jnp.einsum("ijh,jkh->ikh", dx_rows, b_cols, preferred_element_type=jnp.float32)
    piece = dx_rows
    grad_b = lax.psum_scatter(
        jnp.einsum("ijh,ikh->jkh", piece, act_a, preferred_element_type=jnp.float32).astype(
            jnp.bfloat16
        ),
        "row",
        scatter_dimension=0,
        tiled=True,
    ).astype(jnp.float32)
    grad_pair, term_proj = input_back(
        normed_b,
        normed,
        inverse,
        proj,
        pair_mask,
        grad_a,
        grad_b,
        grad_logit,
        ln_in_gain,
        w_proj,
        w_gate,
    )
    sums = lax.psum((term_proj, term_gate, term_out), ("row", "col"))
    scale = 1.0 / total
    return (grad_pair, sums[0] * scale, sums[1] * scale, sums[2] * scale)


def solution(mesh):
    return jax.shard_map(
        body,
        mesh=mesh,
        in_specs=(
            P("row", "col", None),
            P("row", "col", None),
            P(),
            P(),
            P(),
            P(),
            P(),
            P(),
            P(),
            P(),
            P(),
            P(),
        ),
        out_specs=(P("row", "col", None), P(), P(), P()),
        check_vma=False,
    )
```

profile of v0, /device:TPU:0, one launch (start us, length us, event | category | flops | bytes accessed | tf_op | source)
XLA Modules:
  0.0 383.1 jit_solution(8992526114999853381)
XLA Ops:
  7.2 0.0 copy-start
  7.2 0.0 all-gather.3.cloned.1.call-start
  7.2 0.7 convert_element_type.61
  7.9 0.1 dynamic_slice.13
  8.0 0.1 dynamic_slice.12
  8.1 1.4 convert_reduce_fusion
  9.5 1.7 fusion.19
  11.2 0.1 broadcast_multiply_fusion.3
  11.2 2.0 fusion.42
  13.3 1.9 copy-done.1
  15.2 1.4 multiply_convert_fusion.4
  16.6 0.0 all-gather.3.cloned.1.call-update
  16.6 0.0 reduce-scatter.3.cloned.1.call-start
  16.7 1.7 copy.32
  18.4 36.4 %all-gather.3.cloned.1.call-done = bf16[256,32,128]{2,1,0:T(8,128)(2,1)} async-done(((bf16[64,32,128]{2,1,0:T(8,128)(2,1)}), bf16[256,32,128]{2,1,0:T(8,128)(2,1)}) %all-gather.3.cloned.1.call-update) | async-done | bytes 2097168 | tf_op jit(solution)/shard_map/all_gather | solution.py:132
  54.8 3.9 %copy.34 = bf16[256,32,128]{0,1,2:T(8,128)(2,1)S(1)} copy(bf16[256,32,128]{2,1,0:T(8,128)(2,1)} %all-gather.3.cloned.1.call-done) | data formatting | bytes 4194304 | tf_op jit(solution)/shard_map/all_gather | solution.py:132
  58.7 3.3 fusion.59
  62.0 6.9 %copy.33 = bf16[128,256,64]{0,1,2:T(8,128)(2,1)} copy(bf16[128,256,64]{1,2,0:T(8,128)(2,1)} %fusion.59) | data formatting | bytes 8388608 | tf_op jit(solution)/shard_map/ikh,jkh->jih/dot_general | solution.py:136
  68.9 0.0 copy-start.17
  68.9 0.0 reduce-scatter.3.cloned.1.call-update
  69.0 0.0 copy-start.11
  69.0 0.0 copy-start.13
  69.0 0.0 all-gather.5.cloned.1.call-start
  69.0 0.6 copy-done.16
  69.6 0.1 dynamic_slice.15
  69.7 0.1 dynamic_slice.14
  69.7 0.1 compare_convert_fusion
  69.8 2.9 fusion.6
  72.8 46.4 %reduce-scatter.3.cloned.1.call-done = bf16[32,64,128]{2,0,1:T(8,128)(2,1)} async-done(((bf16[256,64,128]{2,0,1:T(8,128)(2,1)}), bf16[32,64,128]{2,0,1:T(8,128)(2,1)}) %reduce-scatter.3.cloned.1.call-update) | async-done | bytes 524304 | tf_op jit(solution)/shard_map/reduce_scatter | solution.py:135
  119.1 1.5 bitcast_reduce_fusion
  120.6 1.7 fusion.38
  122.3 2.7 fusion.58
  125.1 2.0 fusion.35
  127.0 0.0 all-gather.5.cloned.1.call-update
  127.0 0.2 reduce-scatter.5.cloned.1.call-start
  127.3 45.2 %all-gather.5.cloned.1.call-done = bf16[64,256,128]{2,1,0:T(8,128)(2,1)} async-done(((bf16[64,32,128]{2,1,0:T(8,128)(2,1)}), bf16[64,256,128]{2,1,0:T(8,128)(2,1)}) %all-gather.5.cloned.1.call-update) | async-done | bytes 4194320 | tf_op jit(solution)/shard_map/all_gather | solution.py:148
  172.5 15.6 %copy.35 = bf16[64,256,128]{0,1,2:T(8,128)(2,1)} copy(bf16[64,256,128]{2,1,0:T(8,128)(2,1)} %all-gather.5.cloned.1.call-done) | data formatting | bytes 8388608 | tf_op jit(solution)/shard_map/all_gather | solution.py:148
  188.1 7.6 %fusion.61 = bf16[128,32,256]{2,1,0:T(8,128)(2,1)} fusion(bf16[64,32,128]{0,1,2:T(8,128)(2,1)S(1)} %copy.32, bf16[64,256,128]{0,1,2:T(8,128)(2,1)} %copy.35), kind=kOutput, calls=%fused_computation.91 | convolution fusion | flops 134217728 | bytes 6815744 | tf_op jit(solution)/shard_map/ijh,ikh->jkh/dot_general | solution.py:152
  195.7 5.3 %copy.39 = bf16[128,32,256]{0,1,2:T(8,128)(2,1)} copy(bf16[128,32,256]{2,1,0:T(8,128)(2,1)} %fusion.61) | data formatting | bytes 4194304 | tf_op jit(solution)/shard_map/ijh,ikh->jkh/dot_general | solution.py:152
  201.0 0.0 reduce-scatter.5.cloned.1.call-update
  201.0 0.0 all-reduce.3.cloned.1.call-start
  201.1 0.0 copy-done.3
  201.1 0.0 copy-done.18
  201.1 0.0 copy-start.5
  201.1 0.0 copy-start.7
  201.1 2.2 fusion.7
  203.3 0.0 copy-done.4
  203.3 1.6 convolution_bitcast_fusion.2
  204.9 1.6 convolution_bitcast_fusion.1
  206.5 1.3 fusion.46
  207.8 5.9 %fusion.60 = f32[128,32,64]{2,1,0:T(8,128)} fusion(bf16[256,32,128]{0,1,2:T(8,128)(2,1)S(1)} %copy.34, bf16[64,256,128]{0,1,2:T(8,128)(2,1)} %copy.35), kind=kOutput, calls=%fused_computation.90 | convolution fusion | flops 134217728 | bytes 7340032 | tf_op jit(solution)/shard_map/ijh,jkh->ikh/dot_general | solution.py:149
  213.7 3.1 copy.36
  216.8 18.3 %reduce-scatter.5.cloned.1.call-done = bf16[64,32,128]{2,1,0:T(8,128)(2,1)} async-done(((bf16[256,32,128]{2,1,0:T(8,128)(2,1)}), bf16[64,32,128]{2,1,0:T(8,128)(2,1)}) %reduce-scatter.5.cloned.1.call-update) | async-done | bytes 524304 | tf_op jit(solution)/shard_map/reduce_scatter | solution.py:151
  235.1 2.9 multiply_convert_fusion.3
  238.0 0.0 copy-start.9
  238.0 0.8 copy-done.10
  238.7 1.8 convolution_bitcast_fusion
  240.6 2.5 fusion.57
  243.1 0.0 all-reduce.3.cloned.1.call-update
  243.1 1.9 fusion.18
  245.1 126.8 %all-reduce.3.cloned.1.call-done = (f32[128,512]{1,0:T(8,128)}, f32[128,128]{1,0:T(8,128)}, f32[128,128]{1,0:T(8,128)}) async-done(((f32[128,512]{1,0:T(8,128)}, f32[128,128]{1,0:T(8,128)}, f32[128,128]{1,0:T(8,128)}), (f32[128,512]{1,0:T(8,128)}, f32[128,128]{1,0:T(8,128)}, f32[128,128]{1,0:T(8,128)})) %all-reduce.3.cloned.1.call-update) | async-done | bytes 393232 | tf_op jit(solution)/shard_map/psum | solution.py:172
  371.9 1.7 broadcast_multiply_fusion
  373.6 1.5 broadcast_multiply_fusion.2
  375.1 1.5 broadcast_multiply_fusion.1
  (32 shorter events, 0.1 us)
Async XLA Ops:
  7.2 4.1 %copy-start = (bf16[128,512]{1,0:T(8,128)(2,1)S(1)}, bf16[128,512]{1,0:T(8,128)(2,1)}, u32[]{:S(2)}) copy-start(bf16[128,512]{1,0:T(8,128)(2,1)} %param.18) | copy-start | bytes 393220
  7.2 47.6 %all-gather.3.cloned.1.call-start = ((), (), s32[]{:S(2)}) async-start(), calls=%async_computation.2 | async-start | bytes 2621440 | tf_op jit(solution)/shard_map/all_gather | solution.py:132
  13.2 2.0 copy-start.1
  16.6 102.5 %reduce-scatter.3.cloned.1.call-start = ((), (), s32[]{:S(2)}) async-start(), calls=%async_computation.3 | async-start | bytes 4718592 | tf_op jit(solution)/shard_map/reduce_scatter | solution.py:135
  68.9 0.7 copy-start.16
  68.9 0.9 copy-start.12
  68.9 0.9 copy-start.14
  68.9 0.9 copy-start.15
  68.9 0.9 copy-start.17
  69.0 53.3 %copy-start.11 = (bf16[128,128]{1,0:T(8,128)(2,1)S(1)}, bf16[128,128]{1,0:T(8,128)(2,1)}, u32[]{:S(2)}) copy-start(bf16[128,128]{1,0:T(8,128)(2,1)} %param.23) | copy-start | bytes 98308
  69.0 53.3 %copy-start.13 = (f32[128]{0:T(128)S(1)}, f32[128]{0:T(128)}, u32[]{:S(2)}) copy-start(f32[128]{0:T(128)} %param.21) | copy-start | bytes 1540
  69.0 103.5 %all-gather.5.cloned.1.call-start = ((), (), s32[]{:S(2)}) async-start(), calls=%async_computation.4 | async-start | bytes 4718592 | tf_op jit(solution)/shard_map/all_gather | solution.py:148
  119.1 5.9 %copy-start.2 = (bf16[32,64,128]{2,0,1:T(8,128)(2,1)S(1)}, bf16[32,64,128]{2,0,1:T(8,128)(2,1)}, u32[]{:S(2)}) copy-start(bf16[32,64,128]{2,0,1:T(8,128)(2,1)} %reduce-scatter.3.cloned.1.call-done) | copy-start | bytes 1572868
  127.0 108.0 %reduce-scatter.5.cloned.1.call-start = ((), (), s32[]{:S(2)}) async-start(), calls=%async_computation.5 | async-start | bytes 2621440 | tf_op jit(solution)/shard_map/reduce_scatter | solution.py:151
  195.7 5.4 %copy-start.3 = (bf16[32,64,128]{2,0,1:T(8,128)(2,1)S(1)}, bf16[32,64,128]{2,0,1:T(8,128)(2,1)}, u32[]{:S(2)}) copy-start(bf16[32,64,128]{2,0,1:T(8,128)(2,1)} %reduce-scatter.3.cloned.1.call-done) | copy-start | bytes 1572868
  195.7 5.4 %copy-start.18 = (f32[128]{0:T(128)S(1)}, f32[128]{0:T(128)}, u32[]{:S(2)}) copy-start(f32[128]{0:T(128)} %param.22) | copy-start | bytes 1540
  195.7 7.6 %copy-start.4 = (bf16[64,32,128]{2,1,0:T(8,128)(2,1)S(1)}, bf16[64,32,128]{2,1,0:T(8,128)(2,1)}, u32[]{:S(2)}) copy-start(bf16[64,32,128]{2,1,0:T(8,128)(2,1)} %param.12) | copy-start | bytes 1572868
  201.0 170.9 %all-reduce.3.cloned.1.call-start = ((), (), s32[]{:S(2)}) async-start(), calls=%async_computation.6 | async-start | bytes 786432 | tf_op jit(solution)/shard_map/psum | solution.py:172
  201.1 3.8 copy-start.5
  201.1 3.8 copy-start.7
  237.9 0.8 copy-start.10
  238.0 2.6 copy-start.8
  238.0 2.6 copy-start.9
  238.7 1.8 copy-start.6
Sparse Core Ops, SparseCore 0:
  16.7 37.9 all-gather.2
  69.1 49.9 reduce-scatter.2
  127.2 45.2 all-gather.4
  201.1 33.9 reduce-scatter.4
  243.3 128.6 all-reduce.2
where the time goes:
time: 384 us; the launch traced here: 383 us
  waiting for transfers between devices  273 us (71%)
  local copies, waits for them, and re-layouts  40.2 us (10%)
  matrix products  35.4 us (9%)
  other arithmetic  19.8 us (5%)
  between operations  14.1 us (4%)
    psum x1, waiting for transfers between devices, body(): sums = lax.psum((term_proj, term_gate, term_out), ('row', 'col'))  127 us
    reduce_scatter x1, waiting for transfers between devices, body(): lax.psum_scatter(jnp.einsum('ikh,jkh->jih', act_a, piece, preferred_eleme...  46.4 us
    all_gather x1, waiting for transfers between devices, body(): dx_rows = lax.all_gather(grad_mixed, 'col', axis=1, tiled=True)  45.2 us
    all_gather x1, waiting for transfers between devices, body(): b_cols = lax.all_gather(act_b, 'row', axis=0, tiled=True)  36.4 us
    reduce_scatter x1, waiting for transfers between devices, body(): lax.psum_scatter(jnp.einsum('ijh,ikh->jkh', piece, act_a, preferred_eleme...  18.3 us
    all_gather x1, local copies, waits for them, and re-layouts, body(): dx_rows = lax.all_gather(grad_mixed, 'col', axis=1, tiled=True)  15.6 us
    dot_general x6, matrix products, matmul_last(): jnp.dot(left.reshape(-1, shape[-1]), right, preferred_element_type=jnp.fl...  13.7 us
  transfers between devices with their start and end apart: 5, of which 5 were waited for; matrix products, arithmetic and copies ran while one was open for 6% of the time, Pallas kernels for 0%

commit v1 on v0

v1 whole, which is shorter than its diff:
```python
import functools

import jax
import jax.numpy as jnp
from jax import lax
from jax.experimental import pallas as pl
from jax.experimental.pallas import tpu as pltpu
from jax.sharding import PartitionSpec as P

EPS = 1e-05
MESH = pl.DeviceIdType.MESH
F32 = jnp.float32
BF16 = jnp.bfloat16
LANES = 128


def dot(left, right, dims):
    return lax.dot_general(left, right, ((dims[:1], dims[1:]), ((), ())), preferred_element_type=F32)


def mean(values):
    return jnp.mean(values, axis=-1, keepdims=True)


def normalise(values):
    centred = values - mean(values)
    inverse = lax.rsqrt(mean(centred * centred) + EPS)
    return centred * inverse, inverse


def norm_back(grad, normed, inverse):
    return (grad - mean(grad) - normed * mean(grad * normed)) * inverse


def unfold(values, rows):
    parts = values.reshape(-1, 16, LANES)
    return jnp.concatenate([parts[:, :, :rows], parts[:, :, rows:]], axis=1).reshape(-1, rows)


def fold(values, rows):
    parts = values.reshape(-1, 32, rows)
    return jnp.concatenate([parts[:, :16], parts[:, 16:]], axis=2).reshape(-1, LANES)


def kernel(
    nr, nc, rows, cols,
    pair, cot, mask_s, chain_s, mask_v, chain_v, gain_in, bias_in, w_proj, w_gate, chain_bias,
    gain_out, bias_out, w_out,
    out, out_proj, out_gate, out_out,
    in32, cot32, zn_s, normed_s, inv_s, act_s, gate_s, y_s, gu_s, gl_s, gz_s,
    fold_a, fold_b, big32, a_mats, b_mats, g_mats,
    a_send, a_recv, b_send, b_all, m_send, m_recv, g_send, g_recv, ga_send, ga_recv,
    gp_send, gp_recv, gb_send, gb_recv, acc, w_send, w_recv, r_recv, f_recv,
    send_sem, recv_sem, bs_sem, br_sem, ps_sem, pr_sem, rs_sem, rr_sem,
):
    r = lax.axis_index("row")
    c = lax.axis_index("col")
    total = nr * rows
    hc = LANES // nc
    slab = 16 * hc
    full = nc * slab
    steps = 16
    lines = nc * 16

    def mod(value, count):
        return lax.rem(value + count, count)

    def at(ref, start, size):
        return ref.at[pl.ds(pl.multiple_of(start, 16), size)]

    barrier = pltpu.get_barrier_semaphore()
    for o in range(1, nc):
        pl.semaphore_signal(barrier, inc=1, device_id=(r, mod(c + o, nc)), device_id_type=MESH)
    for o in range(1, nr):
        pl.semaphore_signal(barrier, inc=1, device_id=(mod(r + o, nr), c), device_id_type=MESH)

    def col_copy(which, o, src, dst):
        return pltpu.make_async_remote_copy(
            src_ref=src, dst_ref=dst, send_sem=send_sem.at[which, o], recv_sem=recv_sem.at[which, o],
            device_id=(r, mod(c + o, nc)), device_id_type=MESH)

    def scatter(which, src, dst, base=0, size=slab):
        for o in range(1, nc):
            col_copy(which, o, at(src, mod(c + o, nc) * size, size), at(dst, base + c * size, size)).start()
        own = pl.ds(pl.multiple_of(base + c * size, 16), size)
        dst[own, :] = src[pl.ds(pl.multiple_of(c * size, 16), size), :]

    def arrived(which, o, src, dst, base=0, size=slab):
        col_copy(which, o, at(src, 0, size), at(dst, base + mod(c - o, nc) * size, size)).wait_recv()

    def gathered(which, src, dst, base=0, size=slab):
        for o in range(1, nc):
            arrived(which, o, src, dst, base, size)

    def cast(dst, src, count):
        size = 256
        def step(t, carry):
            part = pl.ds(pl.multiple_of(t * size, size), size)
            dst[part, :] = src[part, :].astype(dst.dtype)
            return carry
        lax.fori_loop(0, count // size, step, 0)

    def put_turned(dst, low, values):
        turned = values.T
        for t in range(nc):
            dst[pl.ds(pl.multiple_of((t * 16 + low) * hc, hc), hc), :] = turned[t * hc:(t + 1) * hc]

    def get_turned(src, low):
        parts = [src[pl.ds(pl.multiple_of((t * 16 + low) * hc, hc), hc), :] for t in range(nc)]
        return jnp.concatenate(parts, axis=0).T

    def natural(src, low):
        return jnp.concatenate([src[pl.ds(low, rows, stride=cols), :], src[pl.ds(low + 16, rows, stride=cols), :]], axis=0)

    def here(low):
        return pl.ds(pl.multiple_of(low * LANES, LANES), LANES)

    upper = lax.broadcasted_iota(jnp.int32, (LANES, 1), 0) >= rows
    mask_rows = mask_v[pl.ds(pl.multiple_of(r * rows, rows), rows), :].astype(F32)
    mask_rows = jnp.concatenate([mask_rows, mask_rows], axis=0)
    chain_rows = chain_v[pl.ds(pl.multiple_of(r * rows, rows), rows), :]
    chain_rows = jnp.concatenate([chain_rows, chain_rows], axis=0)

    def pair_mask(low):
        first = mask_s[c * cols + low].astype(F32)
        second = mask_s[c * cols + low + 16].astype(F32)
        return mask_rows * jnp.where(upper, second, first)

    cast(in32, pair, rows * cols)

    def project(low, carry):
        normed, inverse = normalise(natural(in32, low))
        zn = (normed * gain_in[...] + bias_in[...]).astype(BF16)
        zn_s[here(low), :] = zn
        normed_s[here(low), :] = normed
        inv_s[here(low), :] = inverse
        proj = dot(zn, w_proj[...], (1, 0))
        mask = pair_mask(low)
        gate_a = jax.nn.sigmoid(proj[:, :LANES])
        gate_b = jax.nn.sigmoid(proj[:, 2 * LANES:3 * LANES])
        value_a = proj[:, LANES:2 * LANES]
        value_b = proj[:, 3 * LANES:]
        act_s[here(low), :LANES] = gate_a
        act_s[here(low), LANES:2 * LANES] = value_a
        act_s[here(low), 2 * LANES:3 * LANES] = gate_b
        act_s[here(low), 3 * LANES:] = value_b
        put_turned(fold_a, low, gate_a * value_a * mask)
        put_turned(fold_b, low, gate_b * value_b * mask)
        return carry

    lax.fori_loop(0, steps, project, 0)
    cast(b_send, fold_b, full)
    cast(a_send, fold_a, full)
    pl.semaphore_wait(barrier, nc - 1 + nr - 1)

    def row_copy(sems, o, slot, src, dst):
        return pltpu.make_async_remote_copy(
            src_ref=src, dst_ref=dst, send_sem=sems[0].at[o, slot], recv_sem=sems[1].at[o, slot],
            device_id=(mod(r + o, nr), c), device_id_type=MESH)

    b_base = r * full
    scatter(0, b_send, b_all, b_base)
    scatter(1, a_send, a_recv)

    def spread(slot):
        piece = at(b_all, b_base + mod(c - slot, nc) * slab, slab)
        for o in range(1, nr):
            row_copy((bs_sem, br_sem), o, slot, piece, piece).start()

    spread(0)
    for slot in range(1, nc):
        arrived(0, slot, b_send, b_all, b_base)
        spread(slot)

    cast(cot32, cot, rows * cols)

    def gates(low, carry):
        first = chain_s[c * cols + low]
        second = chain_s[c * cols + low + 16]
        same = (chain_rows == jnp.where(upper, second, first)).astype(F32)
        logit = dot(zn_s[here(low), :], w_gate[...], (1, 0)) + same * chain_bias[...]
        gate_s[here(low), :] = jax.nn.sigmoid(logit)
        return carry

    lax.fori_loop(0, steps, gates, 0)

    gathered(1, a_send, a_recv)
    cast(fold_a, a_recv, full)
    for slot in range(nc):
        for o in range(1, nr):
            piece = at(b_all, mod(r - o, nr) * full + mod(c - slot, nc) * slab, slab)
            row_copy((bs_sem, br_sem), o, slot, piece, piece).wait_recv()
    cast(big32, b_all, nr * full)

    def mix(h, carry):
        a_mat = unfold(fold_a[pl.ds(h, lines, stride=hc), :], rows).astype(BF16)
        b_mat = jnp.concatenate(
            [unfold(big32[pl.ds(t * full + h, lines, stride=hc), :], rows) for t in range(nr)], axis=1
        ).astype(BF16)
        a_mats[h] = a_mat
        b_mats[h] = b_mat
        fold_b[pl.ds(h, lines, stride=hc), :] = fold(dot(b_mat, a_mat, (0, 0)), rows)
        return carry

    lax.fori_loop(0, hc, mix, 0)
    cast(m_send, fold_b, full)
    scatter(2, m_send, m_recv)
    acc[...] = jnp.zeros_like(acc)
    gathered(2, m_send, m_recv)
    cast(fold_a, m_recv, full)

    def middle(low, carry):
        normed, inverse = normalise(get_turned(fold_a, low))
        y = (normed * gain_out[...] + bias_out[...]).astype(BF16)
        update = dot(y, w_out[...], (1, 0))
        gate = gate_s[here(low), :]
        cot_here = natural(cot32, low)
        grad_update = (cot_here * gate).astype(BF16)
        y_s[here(low), :] = y
        gu_s[here(low), :] = grad_update
        gl_s[here(low), :] = (cot_here * update * gate * (1.0 - gate)).astype(BF16)
        grad_y = dot(grad_update, w_out[...], (1, 1))
        put_turned(fold_b, low, norm_back(grad_y * gain_out[...], normed, inverse))
        return carry

    lax.fori_loop(0, steps, middle, 0)
    cast(g_send, fold_b, full)
    scatter(3, g_send, g_recv)

    def side_terms(low, carry):
        acc[4 * LANES:5 * LANES, :] += dot(zn_s[here(low), :], gl_s[here(low), :], (0, 0))
        acc[5 * LANES:, :] += dot(y_s[here(low), :], gu_s[here(low), :], (0, 0))
        gz_s[here(low), :] = dot(gl_s[here(low), :], w_gate[...], (1, 1))
        return carry

    lax.fori_loop(0, steps, side_terms, 0)
    gathered(3, g_send, g_recv)
    cast(fold_a, g_recv, full)

    def back_b(h, carry):
        g_mat = unfold(fold_a[pl.ds(h, lines, stride=hc), :], rows).astype(BF16)
        g_mats[h] = g_mat
        grad = dot(a_mats[h], g_mat, (1, 1))
        for t in range(nr):
            big32[pl.ds(t * full + h, lines, stride=hc), :] = fold(grad[:, t * rows:(t + 1) * rows], rows)
        return carry

    lax.fori_loop(0, hc, back_b, 0)
    cast(gp_send, big32, nr * full)
    for slot in range(nc):
        for o in range(1, nr):
            src = at(gp_send, mod(r + o, nr) * full + mod(c + slot, nc) * slab, slab)
            dst = at(gp_recv, o * full + slot * slab, slab)
            row_copy((ps_sem, pr_sem), o, slot, src, dst).start()

    def back_a(h, carry):
        fold_b[pl.ds(h, lines, stride=hc), :] = fold(dot(b_mats[h], g_mats[h], (1, 0)), rows)
        return carry

    lax.fori_loop(0, hc, back_a, 0)
    cast(ga_send, fold_b, full)
    scatter(4, ga_send, ga_recv)

    for slot in list(range(1, nc)) + [0]:
        target = mod(c + slot, nc) * slab
        summed = big32[pl.ds(pl.multiple_of(r * full + target, 16), slab), :]
        for o in range(1, nr):
            piece = at(gp_recv, o * full + slot * slab, slab)
            row_copy((ps_sem, pr_sem), o, slot, piece, piece).wait_recv()
            summed = summed + gp_recv[pl.ds(o * full + slot * slab, slab), :].astype(F32)
        if slot == 0:
            gb_recv[pl.ds(pl.multiple_of(c * slab, 16), slab), :] = summed.astype(BF16)
        else:
            gb_send[pl.ds(pl.multiple_of(target, 16), slab), :] = summed.astype(BF16)
            col_copy(5, slot, at(gb_send, target, slab), at(gb_recv, c * slab, slab)).start()

    def half(low, src, gate_at, block):
        masked = get_turned(src, low) * pair_mask(low)
        gate = act_s[here(low), gate_at:gate_at + LANES]
        value = act_s[here(low), gate_at + LANES:gate_at + 2 * LANES]
        value_grad = masked * gate
        grad_p = jnp.concatenate([value_grad * value * (1.0 - gate), value_grad], axis=1).astype(BF16)
        term = dot(zn_s[here(low), :], grad_p, (0, 0))
        acc[block * LANES:(block + 1) * LANES, :] += term[:, :LANES]
        acc[(block + 1) * LANES:(block + 2) * LANES, :] += term[:, LANES:]
        return gz_s[here(low), :] + dot(grad_p, w_proj[:, gate_at:gate_at + 2 * LANES], (1, 1))

    gathered(4, ga_send, ga_recv)
    cast(fold_a, ga_recv, full)

    def finish_a(low, carry):
        gz_s[here(low), :] = half(low, fold_a, 0, 0)
        return carry

    lax.fori_loop(0, steps, finish_a, 0)
    gathered(5, gb_send, gb_recv)
    cast(fold_b, gb_recv, full)

    def finish_b(low, carry):
        grad = half(low, fold_b, 2 * LANES, 2) * gain_in[...]
        result = norm_back(grad, normed_s[here(low), :], inv_s[here(low), :])
        in32[pl.ds(low, rows, stride=cols), :] = result[:rows]
        in32[pl.ds(low + 16, rows, stride=cols), :] = result[rows:]
        return carry

    lax.fori_loop(0, steps, finish_b, 0)

    share = 6 * LANES // nc
    cast(w_send, acc, 6 * LANES)
    scatter(6, w_send, w_recv, 0, share)
    cast(out, in32, rows * cols)
    gathered(6, w_send, w_recv, 0, share)
    part = w_recv[:share, :].astype(F32)
    for t in range(1, nc):
        part = part + w_recv[t * share:(t + 1) * share, :].astype(F32)
    mine = pl.ds(pl.multiple_of(r * share, 16), share)
    r_recv[mine, :] = part.astype(BF16)
    for o in range(1, nr):
        piece = at(r_recv, r * share, share)
        row_copy((rs_sem, rr_sem), o, 0, piece, piece).start()
    for o in range(1, nr):
        piece = at(r_recv, mod(r - o, nr) * share, share)
        row_copy((rs_sem, rr_sem), o, 0, piece, piece).wait_recv()
    part = r_recv[:share, :].astype(F32)
    for t in range(1, nr):
        part = part + r_recv[t * share:(t + 1) * share, :].astype(F32)
    f_recv[pl.ds(pl.multiple_of(c * share, 16), share), :] = (part * (1.0 / total)).astype(BF16)
    for o in range(1, nc):
        piece = at(f_recv, c * share, share)
        col_copy(7, o, piece, piece).start()
    gathered(7, f_recv, f_recv, 0, share)
    for t in range(4):
        out_proj[:, t * LANES:(t + 1) * LANES] = f_recv[t * LANES:(t + 1) * LANES, :].astype(F32)
    out_gate[...] = f_recv[4 * LANES:5 * LANES, :].astype(F32)
    out_out[...] = f_recv[5 * LANES:, :].astype(F32)

    for o in range(1, nc):
        for which, ref, size in (
            (0, b_send, slab), (1, a_send, slab), (2, m_send, slab), (3, g_send, slab),
            (4, ga_send, slab), (5, gb_send, slab), (6, w_send, share), (7, f_recv, share),
        ):
            col_copy(which, o, at(ref, 0, size), at(ref, 0, size)).wait_send()
    for o in range(1, nr):
        for slot in range(nc):
            row_copy((bs_sem, br_sem), o, slot, at(b_all, 0, slab), at(b_all, 0, slab)).wait_send()
            row_copy((ps_sem, pr_sem), o, slot, at(gp_send, 0, slab), at(gp_send, 0, slab)).wait_send()
        row_copy((rs_sem, rr_sem), o, 0, at(r_recv, 0, share), at(r_recv, 0, share)).wait_send()


def body(
    nr, nc, pair, cotangent, res_mask, chain, ln_in_gain, ln_in_bias, w_proj, w_gate, chain_bias,
    ln_out_gain, ln_out_bias, w_out,
):
    rows, cols, width = pair.shape
    count = rows * cols
    total = nr * rows
    hc = LANES // nc
    full = LANES * 16
    share = 6 * LANES // nc
    vmem = pl.BlockSpec(memory_space=pltpu.VMEM)
    smem = pl.BlockSpec(memory_space=pltpu.SMEM)

    def wide(size, dtype=BF16):
        return pltpu.VMEM((size, LANES), dtype)

    scratch = [
        wide(count, F32), wide(count, F32), wide(count), wide(count, F32), pltpu.VMEM((count, 1), F32),
        pltpu.VMEM((count, 4 * LANES), F32), wide(count, F32), wide(count), wide(count), wide(count), wide(count, F32),
        wide(full, F32), wide(full, F32), wide(nr * full, F32),
        pltpu.VMEM((hc, total, rows), BF16), pltpu.VMEM((hc, total, total), BF16), pltpu.VMEM((hc, total, rows), BF16),
        wide(full), wide(full), wide(full), wide(nr * full), wide(full), wide(full), wide(full), wide(full), wide(full), wide(full),
        wide(nr * full), wide(nr * full), wide(full), wide(full), wide(6 * LANES, F32),
        wide(6 * LANES), wide(6 * LANES), wide(nr * share), wide(6 * LANES),
        pltpu.SemaphoreType.DMA((8, nc)), pltpu.SemaphoreType.DMA((8, nc)),
        pltpu.SemaphoreType.DMA((nr, nc)), pltpu.SemaphoreType.DMA((nr, nc)),
        pltpu.SemaphoreType.DMA((nr, nc)), pltpu.SemaphoreType.DMA((nr, nc)),
        pltpu.SemaphoreType.DMA((nr, 1)), pltpu.SemaphoreType.DMA((nr, 1)),
    ]
    row = lambda values: values.reshape(1, -1)
    grads = pl.pallas_call(
        functools.partial(kernel, nr, nc, rows, cols),
        out_shape=(
            jax.ShapeDtypeStruct((count, width), BF16),
            jax.ShapeDtypeStruct((width, 4 * LANES), F32),
            jax.ShapeDtypeStruct((width, width), F32),
            jax.ShapeDtypeStruct((LANES, width), F32),
        ),
        in_specs=[vmem, vmem, smem, smem] + [vmem] * 10,
        out_specs=(vmem,) * 4,
        scratch_shapes=scratch,
        compiler_params=pltpu.CompilerParams(collective_id=0, has_side_effects=True, vmem_limit_bytes=56 * 2**20),
        cost_estimate=pl.CostEstimate(flops=2 * 10**9, bytes_accessed=4 * 2**20, transcendentals=0),
    )(
        pair.reshape(count, width), cotangent.reshape(count, width), res_mask, chain,
        res_mask.reshape(-1, 1), chain.reshape(-1, 1), row(ln_in_gain), row(ln_in_bias), w_proj, w_gate,
        row(chain_bias), row(ln_out_gain), row(ln_out_bias), w_out,
    )
    return (grads[0].reshape(rows, cols, width),) + tuple(grads[1:])


def solution(mesh):
    split = P("row", "col", None)
    return jax.shard_map(
        functools.partial(body, mesh.shape["row"], mesh.shape["col"]),
        mesh=mesh,
        in_specs=(split, split) + (P(),) * 10,
        out_specs=(split, P(), P(), P()),
        check_vma=False,
    )
```

time: 384 us -> 146 us (0.38)
  waiting for transfers between devices: 273 us -> 0 us
  Pallas kernels: 0 us -> 139 us
  matrix products: 35.4 us -> 0 us
  local copies, waits for them, and re-layouts: 40.2 us -> 6.55 us
  other arithmetic: 19.8 us -> 0 us
  between operations: 14.1 us -> 0.66 us
    pallas_call x0 -> x1, Pallas kernels: none -> 139 us  [body(): pl.pallas_call(functools.partial(kernel, nr, nc, rows, cols), out_shape=(...]
    psum x1 -> x0, waiting for transfers between devices: 127 us -> none  [body(): sums = lax.psum((term_proj, term_gate, term_out), ('row', 'col'))]
    all_gather x2 -> x0, waiting for transfers between devices: 81.6 us -> none  [the longest x1 45.2 us: body(): dx_rows = lax.all_gather(grad_mixed, 'col', axis=1, tiled=True)]
    reduce_scatter x2 -> x0, waiting for transfers between devices: 64.6 us -> none  [the longest x1 46.4 us: body(): lax.psum_scatter(jnp.einsum('ikh,jkh->jih', act_a, piece, preferred_eleme...]
    dot_general x12 -> x0, matrix products: 35.4 us -> none  [the longest x6 13.7 us: matmul_last(): jnp.dot(left.reshape(-1, shape[-1]), right, preferred_element_type=jnp.fl...]
    all_gather x2 -> x0, local copies, waits for them, and re-layouts: 19.6 us -> none  [the longest x1 15.6 us: body(): dx_rows = lax.all_gather(grad_mixed, 'col', axis=1, tiled=True)]
    dot_general x3 -> x0, local copies, waits for them, and re-layouts: 15.3 us -> none  [the longest x1 6.91 us: body(): jnp.einsum('ikh,jkh->jih', act_a, piece, preferred_element_type=jnp.float32)]
    reduce_sum x4 -> x0, other arithmetic: 6.18 us -> none  [the longest x2 3.34 us: layer_norm(): jnp.mean(centred * centred, axis=-1, keepdims=True) + EPS]
  transfers between devices with their start and end apart: 5 -> 0, of which waited for: 5 -> 0; matrix products, arithmetic and copies ran while one was open for 6% -> 0% of each run, Pallas kernels for 0% -> 0%
where the time goes in v1:
time: 146 us
  Pallas kernels  139 us (95%)
  local copies, waits for them, and re-layouts  6.55 us (4%)
    pallas_call x1, Pallas kernels, body(): pl.pallas_call(functools.partial(kernel, nr, nc, rows, cols), out_shape=(...  139 us
    unnamed x14, local copies, waits for them, and re-layouts  4.95 us

profile of v1, /device:TPU:0, one launch (start us, length us, event | category | flops | bytes accessed | tf_op | source)
XLA Modules:
  0.0 146.2 jit_solution(10543556772847878423)
XLA Ops:
  0.6 0.0 copy-start.4
  0.6 0.7 copy-done.4
  1.3 0.0 copy-start.3
  1.3 0.8 copy.17.chain_v
  2.1 0.0 copy-done.3
  2.1 0.8 copy.16.mask_v
  2.9 139.0 %shard_map.147 = (bf16[2048,128]{1,0:T(8,128)(2,1)}, f32[128,512]{1,0:T(8,128)}, f32[128,128]{1,0:T(8,128)}, f32[128,128]{1,0:T(8,128)}) custom-call(bf16[2048,128]{1,0:T(8,128)(2,1)} %bitcast.13, bf16[2048,128]{1,0:T(8,128)(2,1)} %bitcast.14, s32[256]{0:T(256)} %mask_s.1, s32[256]{0:T(256)} %chain_s.1, s32[256,1]{1,0:T(8,128)} %copy.16.mask_v, ...), custom_call_target="tpu_custom_call" | custom-call | flops 2000000000 | bytes 4194304 | tf_op jit(solution)/shard_map/pallas_call | solution.py:380
  141.9 0.0 copy-start
  141.9 1.9 %copy.22 = bf16[64,32,128]{2,1,0:T(8,128)(2,1)} copy(bf16[64,32,128]{2,1,0:T(8,128)(2,1)} %bitcast.10) | data formatting | bytes 1048576
  143.9 0.0 copy-done
  143.9 0.0 copy-start.2
  143.9 0.7 copy.23
  144.6 0.2 copy-done.2
  144.7 0.0 copy-start.1
  144.7 0.6 copy.24
  145.3 0.2 copy-done.1
  145.6 0.6 copy.25
Async XLA Ops:
  0.6 0.7 copy-start.4
  1.3 0.8 copy-start.3
  141.9 1.9 %copy-start = (f32[128,512]{1,0:T(8,128)S(1)}, f32[128,512]{1,0:T(8,128)}, u32[]{:S(2)}) copy-start(f32[128,512]{1,0:T(8,128)} %get-tuple-element.17) | copy-start | bytes 786436
  143.9 0.9 copy-start.2
  144.7 0.9 copy-start.1

commit v2 on v1

v2 whole, which is shorter than its diff:
```python
import functools

import jax
import jax.numpy as jnp
from jax import lax
from jax.experimental import pallas as pl
from jax.experimental.pallas import tpu as pltpu
from jax.sharding import PartitionSpec as P

EPS = 1e-05
MESH = pl.DeviceIdType.MESH
F32 = jnp.float32
BF16 = jnp.bfloat16
LANES = 128
WIDE = 2


def dot(left, right, dims):
    return lax.dot_general(left, right, ((dims[:1], dims[1:]), ((), ())), preferred_element_type=F32)


def mean(values):
    return jnp.mean(values, axis=-1, keepdims=True)


def normalise(values):
    centred = values - mean(values)
    inverse = lax.rsqrt(mean(centred * centred) + EPS)
    return centred * inverse, inverse


def norm_back(grad, normed, inverse):
    return (grad - mean(grad) - normed * mean(grad * normed)) * inverse


def unfold(values, rows):
    parts = values.reshape(-1, 16, LANES)
    return jnp.concatenate([parts[:, :, :rows], parts[:, :, rows:]], axis=1).reshape(-1, rows)


def fold(values, rows):
    parts = values.reshape(-1, 32, rows)
    return jnp.concatenate([parts[:, :16], parts[:, 16:]], axis=2).reshape(-1, LANES)


def kernel(
    nr, nc, rows, cols,
    pair, cot, mask_s, chain_s, mask_v, chain_v, gain_in, bias_in, w_proj, w_gate, chain_bias,
    gain_out, bias_out, w_out,
    out, out_proj, out_gate, out_out,
    in32, cot32, zn_s, normed_s, inv_s, act_s, gate_s, q_s, mid_s, gu_s, gz_s,
    fold_a, fold_b, big32, a_mats, b_mats, g_mats,
    a_send, a_recv, b_send, b_all, m_send, m_recv, g_send, g_recv, ga_send, ga_recv,
    gp_send, gp_recv, gb_send, gb_recv, acc, w_send, w_recv, r_recv, f_recv,
    send_sem, recv_sem, bs_sem, br_sem, ps_sem, pr_sem, rs_sem, rr_sem,
):
    r = lax.axis_index("row")
    c = lax.axis_index("col")
    total = nr * rows
    hc = LANES // nc
    hq = 8
    nh = hc // hq
    slab = 16 * hq
    part = nc * slab
    full = nh * part
    lines = nc * 16

    def mod(value, count):
        return lax.rem(value + count, count)

    def span(start, size):
        return pl.ds(pl.multiple_of(start, 16), size)

    def at(ref, start, size):
        return ref.at[span(start, size)]

    barrier = pltpu.get_barrier_semaphore()
    for o in range(1, nc):
        pl.semaphore_signal(barrier, inc=1, device_id=(r, mod(c + o, nc)), device_id_type=MESH)
    for o in range(1, nr):
        pl.semaphore_signal(barrier, inc=1, device_id=(mod(r + o, nr), c), device_id_type=MESH)

    def col_copy(which, o, src, dst):
        return pltpu.make_async_remote_copy(
            src_ref=src, dst_ref=dst, send_sem=send_sem.at[which, o], recv_sem=recv_sem.at[which, o],
            device_id=(r, mod(c + o, nc)), device_id_type=MESH)

    def scatter(which, src, dst, first=0, base=0, size=slab):
        for o in range(1, nc):
            col_copy(which, o, at(src, first + mod(c + o, nc) * size, size), at(dst, base + c * size, size)).start()
        dst[span(base + c * size, size), :] = src[span(first + c * size, size), :]

    def arrived(which, o, dst, base=0, size=slab):
        piece = at(dst, base + mod(c - o, nc) * size, size)
        col_copy(which, o, piece, piece).wait_recv()

    def gathered(which, dst, base=0, size=slab):
        for o in range(1, nc):
            arrived(which, o, dst, base, size)

    def cast(dst, src, count, start=0):
        size = 256
        def step(t, carry):
            piece = pl.ds(pl.multiple_of(start + t * size, 16), size)
            dst[piece, :] = src[piece, :].astype(dst.dtype)
            return carry
        lax.fori_loop(0, count // size, step, 0)

    def put_turned(dst, step, values):
        for w in range(WIDE):
            turned = values[w * LANES:(w + 1) * LANES].T
            for t in range(nc):
                for half in range(nh):
                    row = ((half * nc + t) * 16 + step * WIDE + w) * hq
                    first = t * hc + half * hq
                    dst[pl.ds(pl.multiple_of(row, 8), hq), :] = turned[first:first + hq]

    def get_turned(src, step):
        blocks = []
        for w in range(WIDE):
            pieces = []
            for t in range(nc):
                for half in range(nh):
                    row = ((half * nc + t) * 16 + step * WIDE + w) * hq
                    pieces.append(src[pl.ds(pl.multiple_of(row, 8), hq), :])
            blocks.append(jnp.concatenate(pieces, axis=0).T)
        return jnp.concatenate(blocks, axis=0)

    def natural(src, step):
        return jnp.concatenate(
            [src[pl.ds(step * WIDE + w + high, rows, stride=cols), :] for w in range(WIDE) for high in (0, 16)], axis=0)

    def here(step):
        return pl.ds(pl.multiple_of(step * WIDE * LANES, LANES), WIDE * LANES)

    def row_values(ref):
        shape = (rows, total)
        wanted = lax.broadcasted_iota(jnp.int32, shape, 0) + r * rows == lax.broadcasted_iota(jnp.int32, shape, 1)
        column = jnp.sum(jnp.where(wanted, ref[...].astype(F32), 0.0), axis=-1, keepdims=True)
        return jnp.concatenate([column] * (2 * WIDE), axis=0)

    position = lax.broadcasted_iota(jnp.int32, (WIDE * 2 * rows, 1), 0) // rows
    mask_rows = row_values(mask_v)
    chain_rows = row_values(chain_v)

    def col_values(ref, step):
        values = jnp.zeros(position.shape, F32)
        for w in range(WIDE):
            for high in range(2):
                scalar = ref[c * cols + step * WIDE + w + 16 * high].astype(F32)
                values = jnp.where(position == 2 * w + high, scalar, values)
        return values

    def pair_mask(step):
        return mask_rows * col_values(mask_s, step)

    def loop(step, count=16 // WIDE):
        def run(t, carry):
            step(t)
            return carry
        lax.fori_loop(0, count, run, 0)

    def activate(step, zn, first, dst):
        proj = dot(zn, w_proj[:, first:first + 2 * LANES], (1, 0))
        gate = jax.nn.sigmoid(proj[:, :LANES])
        value = proj[:, LANES:]
        act_s[here(step), first:first + LANES] = gate
        act_s[here(step), first + LANES:first + 2 * LANES] = value
        put_turned(dst, step, gate * value * pair_mask(step))

    cast(in32, pair, rows * cols)

    def project_b(step):
        normed, inverse = normalise(natural(in32, step))
        zn = (normed * gain_in[...] + bias_in[...]).astype(BF16)
        zn_s[here(step), :] = zn
        normed_s[here(step), :] = normed
        inv_s[here(step), :] = inverse
        activate(step, zn, 2 * LANES, fold_b)

    loop(project_b)
    cast(b_send, fold_b, full)
    pl.semaphore_wait(barrier, nc - 1 + nr - 1)

    def row_copy(sems, o, slot, src, dst):
        return pltpu.make_async_remote_copy(
            src_ref=src, dst_ref=dst, send_sem=sems[0].at[o, slot], recv_sem=sems[1].at[o, slot],
            device_id=(mod(r + o, nr), c), device_id_type=MESH)

    def which(array, half):
        return array * nh + half

    def spread(half, slot):
        piece = at(b_all, r * full + half * part + mod(c - slot, nc) * slab, slab)
        for o in range(1, nr):
            row_copy((bs_sem, br_sem), o, half * nc + slot, piece, piece).start()

    for half in range(nh):
        scatter(which(0, half), b_send, b_all, half * part, r * full + half * part)
        spread(half, 0)

    loop(lambda step: activate(step, zn_s[here(step), :], 0, fold_a))
    cast(a_send, fold_a, full)
    for half in range(nh):
        scatter(which(1, half), a_send, a_recv, half * part, half * part)
    for half in range(nh):
        for slot in range(1, nc):
            arrived(which(0, half), slot, b_all, r * full + half * part)
            spread(half, slot)

    cast(cot32, cot, rows * cols)

    def gates(step):
        same = (chain_rows == col_values(chain_s, step)).astype(F32)
        gate = jax.nn.sigmoid(dot(zn_s[here(step), :], w_gate[...], (1, 0)) + same * chain_bias[...])
        gate_s[here(step), :] = gate
        grad_update = (natural(cot32, step) * gate).astype(BF16)
        gu_s[here(step), :] = grad_update
        q_s[here(step), :] = dot(grad_update, w_out[...], (1, 1)) * gain_out[...]

    loop(gates)
    acc[...] = jnp.zeros_like(acc)

    for half in range(nh):
        gathered(which(1, half), a_recv, half * part)
        cast(fold_a, a_recv, part, half * part)
        for slot in range(nc):
            for o in range(1, nr):
                piece = at(b_all, mod(r - o, nr) * full + half * part + mod(c - slot, nc) * slab, slab)
                row_copy((bs_sem, br_sem), o, half * nc + slot, piece, piece).wait_recv()
        for t in range(nr):
            cast(big32, b_all, part, t * full + half * part)

        def mix(h):
            first = half * part + h
            a_mat = unfold(fold_a[pl.ds(first, lines, stride=hq), :], rows).astype(BF16)
            b_mat = jnp.concatenate(
                [unfold(big32[pl.ds(t * full + first, lines, stride=hq), :], rows) for t in range(nr)], axis=1
            ).astype(BF16)
            a_mats[half * hq + h] = a_mat
            b_mats[half * hq + h] = b_mat
            fold_b[pl.ds(first, lines, stride=hq), :] = fold(dot(a_mat, b_mat, (0, 0)).T, rows)

        loop(mix, hq)
        cast(m_send, fold_b, part, half * part)
        scatter(which(2, half), m_send, m_recv, half * part, half * part)

    for half in range(nh):
        gathered(which(2, half), m_recv, half * part)
        cast(fold_a, m_recv, part, half * part)

    def middle(step):
        normed, inverse = normalise(get_turned(fold_a, step))
        mid_s[here(step), :] = normed
        put_turned(fold_b, step, norm_back(q_s[here(step), :], normed, inverse))

    loop(middle)
    for half in range(nh):
        cast(g_send, fold_b, part, half * part)
        scatter(which(3, half), g_send, g_recv, half * part, half * part)

    def side_terms(step):
        y = (mid_s[here(step), :] * gain_out[...] + bias_out[...]).astype(BF16)
        update = dot(y, w_out[...], (1, 0))
        gate = gate_s[here(step), :]
        grad_logit = (natural(cot32, step) * update * gate * (1.0 - gate)).astype(BF16)
        acc[2 * LANES:3 * LANES, :] += dot(zn_s[here(step), :], grad_logit, (0, 0))
        acc[3 * LANES:4 * LANES, :] += dot(y, gu_s[here(step), :], (0, 0))
        gz_s[here(step), :] = dot(grad_logit, w_gate[...], (1, 1))

    loop(side_terms)

    for half in range(nh):
        gathered(which(3, half), g_recv, half * part)
        cast(fold_a, g_recv, part, half * part)

        def back_b(h):
            first = half * part + h
            g_mat = unfold(fold_a[pl.ds(first, lines, stride=hq), :], rows).astype(BF16)
            g_mats[half * hq + h] = g_mat
            grad = dot(a_mats[half * hq + h], g_mat, (1, 1))
            for t in range(nr):
                big32[pl.ds(t * full + first, lines, stride=hq), :] = fold(grad[:, t * rows:(t + 1) * rows], rows)

        loop(back_b, hq)
        for t in range(nr):
            cast(gp_send, big32, part, t * full + half * part)
        for slot in list(range(1, nc)) + [0]:
            for o in range(1, nr):
                src = at(gp_send, mod(r + o, nr) * full + half * part + mod(c + slot, nc) * slab, slab)
                dst = at(gp_recv, o * full + half * part + slot * slab, slab)
                row_copy((ps_sem, pr_sem), o, half * nc + slot, src, dst).start()

    for half in range(nh):
        def back_a(h):
            index = half * hq + h
            fold_b[pl.ds(half * part + h, lines, stride=hq), :] = fold(dot(b_mats[index], g_mats[index], (1, 0)), rows)

        loop(back_a, hq)
        cast(ga_send, fold_b, part, half * part)
        scatter(which(4, half), ga_send, ga_recv, half * part, half * part)

    def reduce(half):
        for slot in list(range(1, nc)) + [0]:
            target = half * part + mod(c + slot, nc) * slab
            summed = big32[span(r * full + target, slab), :]
            for o in range(1, nr):
                start = o * full + half * part + slot * slab
                row_copy((ps_sem, pr_sem), o, half * nc + slot, at(gp_recv, start, slab), at(gp_recv, start, slab)).wait_recv()
                summed = summed + gp_recv[start:start + slab, :].astype(F32)
            if slot == 0:
                gb_recv[span(target, slab), :] = summed.astype(BF16)
            else:
                gb_send[span(target, slab), :] = summed.astype(BF16)
                col_copy(which(5, half), slot, at(gb_send, target, slab), at(gb_recv, half * part + c * slab, slab)).start()

    def side(step, src, gate_at, block):
        masked = get_turned(src, step) * pair_mask(step)
        gate = act_s[here(step), gate_at:gate_at + LANES]
        value = act_s[here(step), gate_at + LANES:gate_at + 2 * LANES]
        value_grad = masked * gate
        grad_p = jnp.concatenate([value_grad * value * (1.0 - gate), value_grad], axis=1).astype(BF16)
        term = dot(zn_s[here(step), :], grad_p, (0, 0))
        acc[block * LANES:(block + 1) * LANES, :] += term[:, :LANES]
        acc[(block + 1) * LANES:(block + 2) * LANES, :] += term[:, LANES:]
        return gz_s[here(step), :] + dot(grad_p, w_proj[:, gate_at:gate_at + 2 * LANES], (1, 1))

    groups = ((0, 4 * LANES, 0), (4 * LANES, 2 * LANES, 1))

    def terms_out(group):
        first, size, index = groups[group]
        cast(w_send, acc, size, first)
        scatter(6 * nh + index, w_send, w_recv, first, first, size // nc)

    def terms_row(group):
        first, size, index = groups[group]
        share = size // nc
        gathered(6 * nh + index, w_recv, first, share)
        summed = w_recv[first:first + share, :].astype(F32)
        for t in range(1, nc):
            summed = summed + w_recv[first + t * share:first + (t + 1) * share, :].astype(F32)
        base = first // nc * nr
        r_recv[span(base + r * share, share), :] = summed.astype(BF16)
        for o in range(1, nr):
            piece = at(r_recv, base + r * share, share)
            row_copy((rs_sem, rr_sem), o, index, piece, piece).start()

    def terms_back(group):
        first, size, index = groups[group]
        share = size // nc
        base = first // nc * nr
        for o in range(1, nr):
            piece = at(r_recv, base + mod(r - o, nr) * share, share)
            row_copy((rs_sem, rr_sem), o, index, piece, piece).wait_recv()
        summed = r_recv[base:base + share, :].astype(F32)
        for t in range(1, nr):
            summed = summed + r_recv[base + t * share:base + (t + 1) * share, :].astype(F32)
        f_recv[span(first + c * share, share), :] = (summed * (1.0 / total)).astype(BF16)
        for o in range(1, nc):
            piece = at(f_recv, first + c * share, share)
            col_copy(6 * nh + 2 + index, o, piece, piece).start()

    def terms_in(group):
        first, size, index = groups[group]
        gathered(6 * nh + 2 + index, f_recv, first, size // nc)

    reduce(0)
    for half in range(nh):
        gathered(which(4, half), ga_recv, half * part)
        cast(fold_a, ga_recv, part, half * part)

    def finish_a(step):
        gz_s[here(step), :] = side(step, fold_a, 0, 0)

    loop(finish_a)
    for half in range(1, nh):
        reduce(half)
    terms_out(0)
    for half in range(nh):
        gathered(which(5, half), gb_recv, half * part)
        cast(fold_b, gb_recv, part, half * part)

    def finish_b(step):
        grad = side(step, fold_b, 2 * LANES, 4) * gain_in[...]
        result = norm_back(grad, normed_s[here(step), :], inv_s[here(step), :])
        for w in range(WIDE):
            for high in range(2):
                first = (2 * w + high) * rows
                in32[pl.ds(step * WIDE + w + 16 * high, rows, stride=cols), :] = result[first:first + rows]

    loop(finish_b)
    terms_out(1)
    terms_row(0)
    cast(out, in32, rows * cols)
    terms_row(1)
    terms_back(0)
    terms_back(1)
    terms_in(0)
    for t in range(2):
        out_proj[:, t * LANES:(t + 1) * LANES] = f_recv[t * LANES:(t + 1) * LANES, :].astype(F32)
    out_gate[...] = f_recv[2 * LANES:3 * LANES, :].astype(F32)
    out_out[...] = f_recv[3 * LANES:4 * LANES, :].astype(F32)
    terms_in(1)
    for t in range(2, 4):
        out_proj[:, t * LANES:(t + 1) * LANES] = f_recv[(t + 2) * LANES:(t + 3) * LANES, :].astype(F32)

    for o in range(1, nc):
        for array, ref in enumerate((b_send, a_send, m_send, g_send, ga_send, gb_send)):
            for half in range(nh):
                col_copy(which(array, half), o, at(ref, 0, slab), at(ref, 0, slab)).wait_send()
        for first, size, index in groups:
            piece = at(w_send, 0, size // nc)
            col_copy(6 * nh + index, o, piece, piece).wait_send()
            col_copy(6 * nh + 2 + index, o, piece, piece).wait_send()
    for o in range(1, nr):
        for slot in range(nh * nc):
            row_copy((bs_sem, br_sem), o, slot, at(b_all, 0, slab), at(b_all, 0, slab)).wait_send()
            row_copy((ps_sem, pr_sem), o, slot, at(gp_send, 0, slab), at(gp_send, 0, slab)).wait_send()
        for first, size, index in groups:
            piece = at(r_recv, 0, size // nc)
            row_copy((rs_sem, rr_sem), o, index, piece, piece).wait_send()


def body(
    nr, nc, pair, cotangent, res_mask, chain, ln_in_gain, ln_in_bias, w_proj, w_gate, chain_bias,
    ln_out_gain, ln_out_bias, w_out,
):
    rows, cols, width = pair.shape
    count = rows * cols
    total = nr * rows
    hc = LANES // nc
    halves = hc // 8
    full = LANES * 16
    share = 6 * LANES // nc
    vmem = pl.BlockSpec(memory_space=pltpu.VMEM)
    smem = pl.BlockSpec(memory_space=pltpu.SMEM)

    def wide(size, dtype=BF16):
        return pltpu.VMEM((size, LANES), dtype)

    scratch = [
        wide(count, F32), wide(count, F32), wide(count), wide(count, F32), pltpu.VMEM((count, 1), F32),
        pltpu.VMEM((count, 4 * LANES), F32), wide(count, F32), wide(count, F32), wide(count, F32), wide(count), wide(count, F32),
        wide(full, F32), wide(full, F32), wide(nr * full, F32),
        pltpu.VMEM((hc, total, rows), BF16), pltpu.VMEM((hc, total, total), BF16), pltpu.VMEM((hc, total, rows), BF16),
        wide(full), wide(full), wide(full), wide(nr * full), wide(full), wide(full), wide(full), wide(full), wide(full), wide(full),
        wide(nr * full), wide(nr * full), wide(full), wide(full), wide(6 * LANES, F32),
        wide(6 * LANES), wide(6 * LANES), wide(nr * share), wide(6 * LANES),
        pltpu.SemaphoreType.DMA((6 * halves + 4, nc)), pltpu.SemaphoreType.DMA((6 * halves + 4, nc)),
        pltpu.SemaphoreType.DMA((nr, halves * nc)), pltpu.SemaphoreType.DMA((nr, halves * nc)),
        pltpu.SemaphoreType.DMA((nr, halves * nc)), pltpu.SemaphoreType.DMA((nr, halves * nc)),
        pltpu.SemaphoreType.DMA((nr, 2)), pltpu.SemaphoreType.DMA((nr, 2)),
    ]
    row = lambda values: values.reshape(1, -1)
    grads = pl.pallas_call(
        functools.partial(kernel, nr, nc, rows, cols),
        out_shape=(
            jax.ShapeDtypeStruct((count, width), BF16),
            jax.ShapeDtypeStruct((width, 4 * LANES), F32),
            jax.ShapeDtypeStruct((width, width), F32),
            jax.ShapeDtypeStruct((LANES, width), F32),
        ),
        in_specs=[vmem, vmem, smem, smem] + [vmem] * 10,
        out_specs=(vmem,) * 4,
        scratch_shapes=scratch,
        compiler_params=pltpu.CompilerParams(collective_id=0, has_side_effects=True, vmem_limit_bytes=56 * 2**20),
        cost_estimate=pl.CostEstimate(flops=2 * 10**9, bytes_accessed=4 * 2**20, transcendentals=0),
    )(
        pair.reshape(count, width), cotangent.reshape(count, width), res_mask, chain,
        row(res_mask), row(chain), row(ln_in_gain), row(ln_in_bias), w_proj, w_gate,
        row(chain_bias), row(ln_out_gain), row(ln_out_bias), w_out,
    )
    return (grads[0].reshape(rows, cols, width),) + tuple(grads[1:])


def solution(mesh):
    split = P("row", "col", None)
    return jax.shard_map(
        functools.partial(body, mesh.shape["row"], mesh.shape["col"]),
        mesh=mesh,
        in_specs=(split, split) + (P(),) * 10,
        out_specs=(split, P(), P(), P()),
        check_vma=False,
    )
```

time: 146 us -> 119 us (0.82)
  Pallas kernels: 139 us -> 114 us
  local copies, waits for them, and re-layouts: 6.55 us -> 4.27 us
    pallas_call x1, Pallas kernels: 139 us -> 114 us  [body(): pl.pallas_call(functools.partial(kernel, nr, nc, rows, cols), out_shape=(...]
    reshape x2 -> x0, local copies, waits for them, and re-layouts: 1.6 us -> none  [the longest x1 0.8 us: body(): res_mask.reshape(-1, 1)]
    unnamed x14 -> x10, local copies, waits for them, and re-layouts: 4.95 us -> 4.27 us
where the time goes in v2:
time: 119 us
  Pallas kernels  114 us (96%)
  local copies, waits for them, and re-layouts  4.27 us (4%)
    pallas_call x1, Pallas kernels, body(): pl.pallas_call(functools.partial(kernel, nr, nc, rows, cols), out_shape=(...  114 us
    unnamed x10, local copies, waits for them, and re-layouts  4.27 us

profile of v2, /device:TPU:0, one launch (start us, length us, event | category | flops | bytes accessed | tf_op | source)
XLA Modules:
  0.0 119.0 jit_solution(9996764778698962187)
XLA Ops:
  0.6 114.1 %shard_map.147 = (bf16[2048,128]{1,0:T(8,128)(2,1)}, f32[128,512]{1,0:T(8,128)}, f32[128,128]{1,0:T(8,128)}, f32[128,128]{1,0:T(8,128)}) custom-call(bf16[2048,128]{1,0:T(8,128)(2,1)} %bitcast.11, bf16[2048,128]{1,0:T(8,128)(2,1)} %bitcast.12, s32[256]{0:T(256)} %mask_s.1, s32[256]{0:T(256)} %chain_s.1, s32[1,256]{1,0:T(1,128)} %bitcast.13, ...), custom_call_target="tpu_custom_call" | custom-call | flops 2000000000 | bytes 4194304 | tf_op jit(solution)/shard_map/pallas_call | solution.py:455
  114.7 0.0 copy-start
  114.7 1.9 %copy.20 = bf16[64,32,128]{2,1,0:T(8,128)(2,1)} copy(bf16[64,32,128]{2,1,0:T(8,128)(2,1)} %bitcast.10) | data formatting | bytes 1048576
  116.6 0.0 copy-done
  116.6 0.0 copy-start.2
  116.6 0.7 copy.21
  117.4 0.2 copy-done.2
  117.5 0.0 copy-start.1
  117.5 0.6 copy.22
  118.1 0.2 copy-done.1
  118.4 0.6 copy.23
Async XLA Ops:
  114.7 1.9 %copy-start = (f32[128,512]{1,0:T(8,128)S(1)}, f32[128,512]{1,0:T(8,128)}, u32[]{:S(2)}) copy-start(f32[128,512]{1,0:T(8,128)} %get-tuple-element.17) | copy-start | bytes 786436
  116.6 0.9 copy-start.2
  117.5 0.9 copy-start.1

commit v3 on v2

v3 whole, which is shorter than its diff:
```python
import functools

import jax
import jax.numpy as jnp
from jax import lax
from jax.experimental import pallas as pl
from jax.experimental.pallas import tpu as pltpu
from jax.sharding import PartitionSpec as P

EPS = 1e-05
MESH = pl.DeviceIdType.MESH
F32 = jnp.float32
BF16 = jnp.bfloat16
LANES = 128
WIDE = 2


def dot(left, right, dims):
    return lax.dot_general(left, right, ((dims[:1], dims[1:]), ((), ())), preferred_element_type=F32)


def mean(values):
    return jnp.mean(values, axis=-1, keepdims=True)


def normalise(values):
    centred = values - mean(values)
    inverse = lax.rsqrt(mean(centred * centred) + EPS)
    return centred * inverse, inverse


def norm_back(grad, normed, inverse):
    return (grad - mean(grad) - normed * mean(grad * normed)) * inverse


def unfold(values, rows):
    parts = values.reshape(-1, 16, LANES)
    return jnp.concatenate([parts[:, :, :rows], parts[:, :, rows:]], axis=1).reshape(-1, rows)


def fold(values, rows):
    parts = values.reshape(-1, 32, rows)
    return jnp.concatenate([parts[:, :16], parts[:, 16:]], axis=2).reshape(-1, LANES)


def kernel(
    nr, nc, rows, cols,
    pair, cot, mask_s, chain_s, mask_v, chain_v, gain_in, bias_in, w_proj, w_gate, chain_bias,
    gain_out, bias_out, w_out,
    out, out_proj, out_gate, out_out,
    in32, cot32, zn_s, normed_s, inv_s, act_s, gate_s, q_s, mid_s, gu_s, gz_s,
    fold_a, fold_b, fold_c, a_mats, b_mats, g_mats,
    a_send, a_recv, b_send, b_recv, m_send, m_recv, g_send, g_recv, ga_send, ga_recv,
    gb_send, gb_recv, acc, w_send, w_recv, r_recv, f_recv,
    send_sem, recv_sem, ts_sem, tr_sem, rs_sem, rr_sem,
):
    r = lax.axis_index("row")
    c = lax.axis_index("col")
    total = nr * rows
    nd = nr * nc
    me = r * nc + c
    hq = LANES // nd
    slab = 16 * hq
    part = nc * slab
    full = nd * slab
    lines = nc * 16

    def mod(value, count):
        return lax.rem(value + count, count)

    def span(start, size):
        return pl.ds(pl.multiple_of(start, 16), size)

    def at(ref, start, size):
        return ref.at[span(start, size)]

    barrier = pltpu.get_barrier_semaphore()
    def peer(o):
        other = mod(me + o, nd)
        return (other // nc, other % nc)

    def greet(o, carry):
        pl.semaphore_signal(barrier, inc=1, device_id=peer(o), device_id_type=MESH)
        return carry

    lax.fori_loop(1, nd, greet, 0)

    def copy(array, o, src, dst):
        return pltpu.make_async_remote_copy(
            src_ref=src, dst_ref=dst, send_sem=send_sem.at[array, o], recv_sem=recv_sem.at[array, o],
            device_id=peer(o), device_id_type=MESH)

    def exchange(array, src, dst):
        def send(o, carry):
            copy(array, o, at(src, mod(me + o, nd) * slab, slab), at(dst, me * slab, slab)).start()
            return carry
        lax.fori_loop(1, nd, send, 0)
        dst[span(me * slab, slab), :] = src[span(me * slab, slab), :]

    def arrive(array, dst):
        def take(o, carry):
            piece = at(dst, mod(me - o, nd) * slab, slab)
            copy(array, o, piece, piece).wait_recv()
            return carry
        lax.fori_loop(1, nd, take, 0)

    def col_copy(which, o, src, dst):
        return pltpu.make_async_remote_copy(
            src_ref=src, dst_ref=dst, send_sem=ts_sem.at[which, o], recv_sem=tr_sem.at[which, o],
            device_id=(r, mod(c + o, nc)), device_id_type=MESH)

    def scatter(which, src, dst, first, base, size):
        for o in range(1, nc):
            col_copy(which, o, at(src, first + mod(c + o, nc) * size, size), at(dst, base + c * size, size)).start()
        dst[span(base + c * size, size), :] = src[span(first + c * size, size), :]

    def gathered(which, dst, base, size):
        for o in range(1, nc):
            piece = at(dst, base + mod(c - o, nc) * size, size)
            col_copy(which, o, piece, piece).wait_recv()

    def cast(dst, src, count, start=0):
        size = 256
        def step(t, carry):
            piece = pl.ds(pl.multiple_of(start + t * size, 16), size)
            dst[piece, :] = src[piece, :].astype(dst.dtype)
            return carry
        lax.fori_loop(0, count // size, step, 0)

    def put_turned(dst, step, values):
        turned = [values[w * LANES:(w + 1) * LANES].T for w in range(WIDE)]
        for t in range(nd):
            row = pl.multiple_of((t * 16 + step * WIDE) * hq, WIDE * hq)
            dst[pl.ds(row, WIDE * hq), :] = jnp.concatenate([block[t * hq:(t + 1) * hq] for block in turned], axis=0)

    def get_turned(src, step):
        pieces = [
            src[pl.ds(pl.multiple_of((t * 16 + step * WIDE) * hq, WIDE * hq), WIDE * hq), :] for t in range(nd)
        ]
        blocks = [jnp.concatenate([piece[w * hq:(w + 1) * hq] for piece in pieces], axis=0).T for w in range(WIDE)]
        return jnp.concatenate(blocks, axis=0)

    def matrix(src, h):
        return jnp.concatenate(
            [unfold(src[pl.ds(t * part + h, lines, stride=hq), :], rows) for t in range(nr)], axis=1).astype(BF16)

    def put_matrix(dst, h, values):
        for t in range(nr):
            dst[pl.ds(t * part + h, lines, stride=hq), :] = fold(values[:, t * rows:(t + 1) * rows], rows)

    def natural(src, step):
        return jnp.concatenate(
            [src[pl.ds(step * WIDE + w + high, rows, stride=cols), :] for w in range(WIDE) for high in (0, 16)], axis=0)

    def here(step):
        return pl.ds(pl.multiple_of(step * WIDE * LANES, LANES), WIDE * LANES)

    def row_values(ref):
        shape = (rows, total)
        wanted = lax.broadcasted_iota(jnp.int32, shape, 0) + r * rows == lax.broadcasted_iota(jnp.int32, shape, 1)
        column = jnp.sum(jnp.where(wanted, ref[...].astype(F32), 0.0), axis=-1, keepdims=True)
        return jnp.concatenate([column] * (2 * WIDE), axis=0)

    position = lax.broadcasted_iota(jnp.int32, (WIDE * 2 * rows, 1), 0) // rows
    mask_rows = row_values(mask_v)
    chain_rows = row_values(chain_v)

    def col_values(ref, step):
        values = jnp.zeros(position.shape, F32)
        for w in range(WIDE):
            for high in range(2):
                scalar = ref[c * cols + step * WIDE + w + 16 * high].astype(F32)
                values = jnp.where(position == 2 * w + high, scalar, values)
        return values

    def pair_mask(step):
        return mask_rows * col_values(mask_s, step)

    def loop(step, count=16 // WIDE):
        def run(t, carry):
            step(t)
            return carry
        lax.fori_loop(0, count, run, 0)

    def activate(step, zn, first, dst):
        proj = dot(zn, w_proj[:, first:first + 2 * LANES], (1, 0))
        gate = jax.nn.sigmoid(proj[:, :LANES])
        value = proj[:, LANES:]
        act_s[here(step), first:first + LANES] = gate
        act_s[here(step), first + LANES:first + 2 * LANES] = value
        put_turned(dst, step, gate * value * pair_mask(step))

    cast(in32, pair, rows * cols)

    def project_b(step):
        normed, inverse = normalise(natural(in32, step))
        zn = (normed * gain_in[...] + bias_in[...]).astype(BF16)
        zn_s[here(step), :] = zn
        normed_s[here(step), :] = normed
        inv_s[here(step), :] = inverse
        activate(step, zn, 2 * LANES, fold_b)

    loop(project_b)
    cast(b_send, fold_b, full)
    pl.semaphore_wait(barrier, nd - 1)

    exchange(0, b_send, b_recv)

    def row_copy(sems, o, slot, src, dst):
        return pltpu.make_async_remote_copy(
            src_ref=src, dst_ref=dst, send_sem=sems[0].at[o, slot], recv_sem=sems[1].at[o, slot],
            device_id=(mod(r + o, nr), c), device_id_type=MESH)

    loop(lambda step: activate(step, zn_s[here(step), :], 0, fold_a))
    cast(a_send, fold_a, full)
    exchange(1, a_send, a_recv)
    cast(cot32, cot, rows * cols)

    def gates(step):
        same = (chain_rows == col_values(chain_s, step)).astype(F32)
        gate = jax.nn.sigmoid(dot(zn_s[here(step), :], w_gate[...], (1, 0)) + same * chain_bias[...])
        gate_s[here(step), :] = gate
        grad_update = (natural(cot32, step) * gate).astype(BF16)
        gu_s[here(step), :] = grad_update
        q_s[here(step), :] = dot(grad_update, w_out[...], (1, 1)) * gain_out[...]

    loop(gates)
    acc[...] = jnp.zeros_like(acc)

    arrive(0, b_recv)
    cast(fold_b, b_recv, full)
    arrive(1, a_recv)
    cast(fold_a, a_recv, full)

    def mix(h):
        a_mat = matrix(fold_a, h)
        b_mat = matrix(fold_b, h)
        a_mats[h] = a_mat
        b_mats[h] = b_mat
        put_matrix(fold_c, h, dot(b_mat, a_mat, (0, 0)))

    loop(mix, hq)
    cast(m_send, fold_c, full)
    exchange(2, m_send, m_recv)
    arrive(2, m_recv)
    cast(fold_a, m_recv, full)

    def middle(step):
        normed, inverse = normalise(get_turned(fold_a, step))
        mid_s[here(step), :] = normed
        put_turned(fold_b, step, norm_back(q_s[here(step), :], normed, inverse))

    loop(middle)
    cast(g_send, fold_b, full)
    exchange(3, g_send, g_recv)

    def side_terms(step):
        y = (mid_s[here(step), :] * gain_out[...] + bias_out[...]).astype(BF16)
        update = dot(y, w_out[...], (1, 0))
        gate = gate_s[here(step), :]
        grad_logit = (natural(cot32, step) * update * gate * (1.0 - gate)).astype(BF16)
        acc[2 * LANES:3 * LANES, :] += dot(zn_s[here(step), :], grad_logit, (0, 0))
        acc[3 * LANES:4 * LANES, :] += dot(y, gu_s[here(step), :], (0, 0))
        gz_s[here(step), :] = dot(grad_logit, w_gate[...], (1, 1))

    loop(side_terms)

    arrive(3, g_recv)
    cast(fold_a, g_recv, full)

    def back_a(h):
        g_mat = matrix(fold_a, h)
        g_mats[h] = g_mat
        put_matrix(fold_c, h, dot(b_mats[h], g_mat, (1, 0)))

    loop(back_a, hq)
    cast(ga_send, fold_c, full)
    exchange(4, ga_send, ga_recv)
    loop(lambda h: put_matrix(fold_b, h, dot(a_mats[h], g_mats[h], (1, 1))), hq)
    cast(gb_send, fold_b, full)
    exchange(5, gb_send, gb_recv)

    def side(step, src, gate_at, block):
        masked = get_turned(src, step) * pair_mask(step)
        gate = act_s[here(step), gate_at:gate_at + LANES]
        value = act_s[here(step), gate_at + LANES:gate_at + 2 * LANES]
        value_grad = masked * gate
        grad_p = jnp.concatenate([value_grad * value * (1.0 - gate), value_grad], axis=1).astype(BF16)
        term = dot(zn_s[here(step), :], grad_p, (0, 0))
        acc[block * LANES:(block + 1) * LANES, :] += term[:, :LANES]
        acc[(block + 1) * LANES:(block + 2) * LANES, :] += term[:, LANES:]
        return gz_s[here(step), :] + dot(grad_p, w_proj[:, gate_at:gate_at + 2 * LANES], (1, 1))

    groups = ((0, 4 * LANES, 0), (4 * LANES, 2 * LANES, 1))

    def terms_out(group):
        first, size, index = groups[group]
        cast(w_send, acc, size, first)
        scatter(index, w_send, w_recv, first, first, size // nc)

    def terms_row(group):
        first, size, index = groups[group]
        share = size // nc
        gathered(index, w_recv, first, share)
        summed = w_recv[first:first + share, :].astype(F32)
        for t in range(1, nc):
            summed = summed + w_recv[first + t * share:first + (t + 1) * share, :].astype(F32)
        base = first // nc * nr
        r_recv[span(base + r * share, share), :] = summed.astype(BF16)
        for o in range(1, nr):
            piece = at(r_recv, base + r * share, share)
            row_copy((rs_sem, rr_sem), o, index, piece, piece).start()

    def terms_back(group):
        first, size, index = groups[group]
        share = size // nc
        base = first // nc * nr
        for o in range(1, nr):
            piece = at(r_recv, base + mod(r - o, nr) * share, share)
            row_copy((rs_sem, rr_sem), o, index, piece, piece).wait_recv()
        summed = r_recv[base:base + share, :].astype(F32)
        for t in range(1, nr):
            summed = summed + r_recv[base + t * share:base + (t + 1) * share, :].astype(F32)
        f_recv[span(first + c * share, share), :] = (summed * (1.0 / total)).astype(BF16)
        for o in range(1, nc):
            piece = at(f_recv, first + c * share, share)
            col_copy(2 + index, o, piece, piece).start()

    def terms_in(group):
        first, size, index = groups[group]
        gathered(2 + index, f_recv, first, size // nc)

    arrive(4, ga_recv)
    cast(fold_a, ga_recv, full)

    def finish_a(step):
        gz_s[here(step), :] = side(step, fold_a, 0, 0)

    loop(finish_a)
    terms_out(0)
    arrive(5, gb_recv)
    cast(fold_b, gb_recv, full)

    def finish_b(step):
        grad = side(step, fold_b, 2 * LANES, 4) * gain_in[...]
        result = norm_back(grad, normed_s[here(step), :], inv_s[here(step), :])
        for w in range(WIDE):
            for high in range(2):
                first = (2 * w + high) * rows
                in32[pl.ds(step * WIDE + w + 16 * high, rows, stride=cols), :] = result[first:first + rows]

    loop(finish_b)
    terms_out(1)
    terms_row(0)
    cast(out, in32, rows * cols)
    terms_row(1)
    terms_back(0)
    terms_back(1)
    terms_in(0)
    for t in range(2):
        out_proj[:, t * LANES:(t + 1) * LANES] = f_recv[t * LANES:(t + 1) * LANES, :].astype(F32)
    out_gate[...] = f_recv[2 * LANES:3 * LANES, :].astype(F32)
    out_out[...] = f_recv[3 * LANES:4 * LANES, :].astype(F32)
    terms_in(1)
    for t in range(2, 4):
        out_proj[:, t * LANES:(t + 1) * LANES] = f_recv[(t + 2) * LANES:(t + 3) * LANES, :].astype(F32)

    def sent(o, carry):
        for array, ref in enumerate((b_send, a_send, m_send, g_send, ga_send, gb_send)):
            copy(array, o, at(ref, 0, slab), at(ref, 0, slab)).wait_send()
        return carry

    lax.fori_loop(1, nd, sent, 0)
    for first, size, index in groups:
        for o in range(1, nc):
            piece = at(w_send, 0, size // nc)
            col_copy(index, o, piece, piece).wait_send()
            col_copy(2 + index, o, piece, piece).wait_send()
        for o in range(1, nr):
            piece = at(r_recv, 0, size // nc)
            row_copy((rs_sem, rr_sem), o, index, piece, piece).wait_send()


def body(
    nr, nc, pair, cotangent, res_mask, chain, ln_in_gain, ln_in_bias, w_proj, w_gate, chain_bias,
    ln_out_gain, ln_out_bias, w_out,
):
    rows, cols, width = pair.shape
    count = rows * cols
    total = nr * rows
    hq = LANES // (nr * nc)
    full = LANES * 16
    share = 6 * LANES // nc
    vmem = pl.BlockSpec(memory_space=pltpu.VMEM)
    smem = pl.BlockSpec(memory_space=pltpu.SMEM)

    def wide(size, dtype=BF16):
        return pltpu.VMEM((size, LANES), dtype)

    scratch = [
        wide(count, F32), wide(count, F32), wide(count), wide(count, F32), pltpu.VMEM((count, 1), F32),
        pltpu.VMEM((count, 4 * LANES), F32), wide(count, F32), wide(count, F32), wide(count, F32), wide(count), wide(count, F32),
        wide(full, F32), wide(full, F32), wide(full, F32),
        pltpu.VMEM((hq, total, total), BF16), pltpu.VMEM((hq, total, total), BF16), pltpu.VMEM((hq, total, total), BF16),
        wide(full), wide(full), wide(full), wide(full), wide(full), wide(full), wide(full), wide(full), wide(full), wide(full), wide(full), wide(full), wide(6 * LANES, F32),
        wide(6 * LANES), wide(6 * LANES), wide(nr * share), wide(6 * LANES),
        pltpu.SemaphoreType.DMA((6, nr * nc)), pltpu.SemaphoreType.DMA((6, nr * nc)),
        pltpu.SemaphoreType.DMA((4, nc)), pltpu.SemaphoreType.DMA((4, nc)),
        pltpu.SemaphoreType.DMA((nr, 2)), pltpu.SemaphoreType.DMA((nr, 2)),
    ]
    row = lambda values: values.reshape(1, -1)
    grads = pl.pallas_call(
        functools.partial(kernel, nr, nc, rows, cols),
        out_shape=(
            jax.ShapeDtypeStruct((count, width), BF16),
            jax.ShapeDtypeStruct((width, 4 * LANES), F32),
            jax.ShapeDtypeStruct((width, width), F32),
            jax.ShapeDtypeStruct((LANES, width), F32),
        ),
        in_specs=[vmem, vmem, smem, smem] + [vmem] * 10,
        out_specs=(vmem,) * 4,
        scratch_shapes=scratch,
        compiler_params=pltpu.CompilerParams(collective_id=0, has_side_effects=True, vmem_limit_bytes=56 * 2**20),
        cost_estimate=pl.CostEstimate(flops=2 * 10**9, bytes_accessed=4 * 2**20, transcendentals=0),
    )(
        pair.reshape(count, width), cotangent.reshape(count, width), res_mask, chain,
        row(res_mask), row(chain), row(ln_in_gain), row(ln_in_bias), w_proj, w_gate,
        row(chain_bias), row(ln_out_gain), row(ln_out_bias), w_out,
    )
    return (grads[0].reshape(rows, cols, width),) + tuple(grads[1:])


def solution(mesh):
    split = P("row", "col", None)
    return jax.shard_map(
        functools.partial(body, mesh.shape["row"], mesh.shape["col"]),
        mesh=mesh,
        in_specs=(split, split) + (P(),) * 10,
        out_specs=(split, P(), P(), P()),
        check_vma=False,
    )
```

time: 119 us -> 119 us (level)
  no operation moved by 1% of the time
where the time goes in v3:
time: 119 us; the launch traced here: 118 us
  Pallas kernels  113 us (95%)
  local copies, waits for them, and re-layouts  4.27 us (4%)
    pallas_call x1, Pallas kernels, body(): pl.pallas_call(functools.partial(kernel, nr, nc, rows, cols), out_shape=(...  113 us
    unnamed x10, local copies, waits for them, and re-layouts  4.27 us

profile of v3, /device:TPU:0, one launch (start us, length us, event | category | flops | bytes accessed | tf_op | source)
XLA Modules:
  0.0 118.4 jit_solution(15786878058204369905)
XLA Ops:
  0.6 113.5 %shard_map.147 = (bf16[2048,128]{1,0:T(8,128)(2,1)}, f32[128,512]{1,0:T(8,128)}, f32[128,128]{1,0:T(8,128)}, f32[128,128]{1,0:T(8,128)}) custom-call(bf16[2048,128]{1,0:T(8,128)(2,1)} %bitcast.11, bf16[2048,128]{1,0:T(8,128)(2,1)} %bitcast.12, s32[256]{0:T(256)} %mask_s.1, s32[256]{0:T(256)} %chain_s.1, s32[1,256]{1,0:T(1,128)} %bitcast.13, ...), custom_call_target="tpu_custom_call" | custom-call | flops 2000000000 | bytes 4194304 | tf_op jit(solution)/shard_map/pallas_call | solution.py:412
  114.1 0.0 copy-start
  114.1 1.9 %copy.20 = bf16[64,32,128]{2,1,0:T(8,128)(2,1)} copy(bf16[64,32,128]{2,1,0:T(8,128)(2,1)} %bitcast.10) | data formatting | bytes 1048576
  116.1 0.0 copy-done
  116.1 0.0 copy-start.2
  116.1 0.7 copy.21
  116.8 0.2 copy-done.2
  116.9 0.0 copy-start.1
  116.9 0.6 copy.22
  117.6 0.2 copy-done.1
  117.8 0.6 copy.23
Async XLA Ops:
  114.1 1.9 %copy-start = (f32[128,512]{1,0:T(8,128)S(1)}, f32[128,512]{1,0:T(8,128)}, u32[]{:S(2)}) copy-start(f32[128,512]{1,0:T(8,128)} %get-tuple-element.17) | copy-start | bytes 786436
  116.1 0.9 copy-start.2
  116.9 0.9 copy-start.1

commit v4 on v3

--- a/solution.py
+++ b/solution.py
@@ -12,7 +12,7 @@
 F32 = jnp.float32
 BF16 = jnp.bfloat16
 LANES = 128
-WIDE = 2
+WIDE = 4
 
 
 def dot(left, right, dims):
@@ -176,11 +176,11 @@
     def pair_mask(step):
         return mask_rows * col_values(mask_s, step)
 
-    def loop(step, count=16 // WIDE):
+    def loop(step, count=16 // WIDE, unroll=1):
         def run(t, carry):
             step(t)
             return carry
-        lax.fori_loop(0, count, run, 0)
+        lax.fori_loop(0, count, run, 0, unroll=unroll)
 
     def activate(step, zn, first, dst):
         proj = dot(zn, w_proj[:, first:first + 2 * LANES], (1, 0))
@@ -239,7 +239,7 @@
         b_mats[h] = b_mat
         put_matrix(fold_c, h, dot(b_mat, a_mat, (0, 0)))
 
-    loop(mix, hq)
+    loop(mix, hq, min(hq, 4))
     cast(m_send, fold_c, full)
     exchange(2, m_send, m_recv)
     arrive(2, m_recv)
@@ -273,10 +273,10 @@
         g_mats[h] = g_mat
         put_matrix(fold_c, h, dot(b_mats[h], g_mat, (1, 0)))
 
-    loop(back_a, hq)
+    loop(back_a, hq, min(hq, 4))
     cast(ga_send, fold_c, full)
     exchange(4, ga_send, ga_recv)
-    loop(lambda h: put_matrix(fold_b, h, dot(a_mats[h], g_mats[h], (1, 1))), hq)
+    loop(lambda h: put_matrix(fold_b, h, dot(a_mats[h], g_mats[h], (1, 1))), hq, min(hq, 4))
     cast(gb_send, fold_b, full)
     exchange(5, gb_send, gb_recv)
 
@@ -347,12 +347,11 @@
         for w in range(WIDE):
             for high in range(2):
                 first = (2 * w + high) * rows
-                in32[pl.ds(step * WIDE + w + 16 * high, rows, stride=cols), :] = result[first:first + rows]
+                out[pl.ds(step * WIDE + w + 16 * high, rows, stride=cols), :] = result[first:first + rows]
 
     loop(finish_b)
     terms_out(1)
     terms_row(0)
-    cast(out, in32, rows * cols)
     terms_row(1)
     terms_back(0)
     terms_back(1)
@@ -412,7 +411,7 @@
     grads = pl.pallas_call(
         functools.partial(kernel, nr, nc, rows, cols),
         out_shape=(
-            jax.ShapeDtypeStruct((count, width), BF16),
+            jax.ShapeDtypeStruct((count, width), F32),
             jax.ShapeDtypeStruct((width, 4 * LANES), F32),
             jax.ShapeDtypeStruct((width, width), F32),
             jax.ShapeDtypeStruct((LANES, width), F32),
@@ -427,7 +426,7 @@
         row(res_mask), row(chain), row(ln_in_gain), row(ln_in_bias), w_proj, w_gate,
         row(chain_bias), row(ln_out_gain), row(ln_out_bias), w_out,
     )
-    return (grads[0].reshape(rows, cols, width),) + tuple(grads[1:])
+    return (grads[0].astype(BF16).reshape(rows, cols, width),) + tuple(grads[1:])
 
 
 def solution(mesh):

time: 119 us -> 116 us (0.975)
  Pallas kernels: 113 us -> 110 us
  other arithmetic: 0 us -> 2.11 us
  local copies, waits for them, and re-layouts: 4.27 us -> 2.36 us
    pallas_call x1, Pallas kernels: 113 us -> 110 us  [body(): pl.pallas_call(functools.partial(kernel, nr, nc, rows, cols), out_shape=(...]
    convert_element_type x0 -> x1, other arithmetic: none -> 2.11 us  [body(): grads[0].astype(BF16).reshape(rows, cols, width)]
    unnamed x10 -> x9, local copies, waits for them, and re-layouts: 4.27 us -> 2.36 us
where the time goes in v4:
time: 116 us; the launch traced here: 115 us
  Pallas kernels  110 us (95%)
  local copies, waits for them, and re-layouts  2.36 us (2%)
  other arithmetic  2.11 us (2%)
    pallas_call x1, Pallas kernels, body(): pl.pallas_call(functools.partial(kernel, nr, nc, rows, cols), out_shape=(...  110 us
    unnamed x9, local copies, waits for them, and re-layouts  2.36 us

profile of v4, /device:TPU:0, one launch (start us, length us, event | category | flops | bytes accessed | tf_op | source)
XLA Modules:
  0.0 115.4 jit_solution(15999684707885662894)
XLA Ops:
  0.6 110.3 %shard_map.147 = (f32[2048,128]{1,0:T(8,128)}, f32[128,512]{1,0:T(8,128)}, f32[128,128]{1,0:T(8,128)}, f32[128,128]{1,0:T(8,128)}) custom-call(bf16[2048,128]{1,0:T(8,128)(2,1)} %bitcast.11, bf16[2048,128]{1,0:T(8,128)(2,1)} %bitcast.12, s32[256]{0:T(256)} %mask_s.1, s32[256]{0:T(256)} %chain_s.1, s32[1,256]{1,0:T(1,128)} %bitcast.13, s32[1,256]{1,0:T(1,128)} %bitcast.14, ...), custom_call_target="tpu_custom_call" | custom-call | flops 2000000000 | bytes 4194304 | tf_op jit(solution)/shard_map/pallas_call | solution.py:411
  110.9 0.0 copy-start
  111.0 2.1 %convert_element_type.3 = bf16[2048,128]{1,0:T(8,128)(2,1)} convert(f32[2048,128]{1,0:T(8,128)} %get-tuple-element.8) | non-fusion elementwise | flops 262144 | bytes 1572864 | tf_op jit(solution)/shard_map/convert_element_type | solution.py:429
  113.1 0.0 copy-done
  113.1 0.0 copy-start.2
  113.1 0.7 copy.19
  113.8 0.2 copy-done.2
  113.9 0.0 copy-start.1
  113.9 0.6 copy.20
  114.6 0.2 copy-done.1
  114.8 0.6 copy.21
Async XLA Ops:
  110.9 2.1 %copy-start = (f32[128,512]{1,0:T(8,128)S(1)}, f32[128,512]{1,0:T(8,128)}, u32[]{:S(2)}) copy-start(f32[128,512]{1,0:T(8,128)} %get-tuple-element.17) | copy-start | bytes 786436
  113.1 0.9 copy-start.2
  113.9 0.9 copy-start.1
